TPU v7x, 256 devices: a whole 4x4x8 slice. The times are simulated.
256 devices in a mesh: grp: 16 (over x, y_lo, core), tp: 16 (over z, y_hi).
Axes of the slice: x: 4, y: 4 (y_hi: 2, y_lo: 2; y = y_hi * 2 + y_lo), z: 8, core: 2. Of those that a mesh axis runs over, the one named last changes fastest.
Arguments:
- hidden: bfloat16 [2, 32768, 8192], P(None, ('grp', 'tp')), may hold values from -6 to 6
- norm_gain: float32 [8192], replicated, may hold values from 0.1 to 1.9
- kv_weight: bfloat16 [8192, 1024], P(('grp', 'tp')), may hold values from -0.0625 to 0.0625
- queries: bfloat16 [2, 32768, 4096], P(None, 'grp', 'tp'), may hold values from -512 to 512
- positions: int32 [32768], P(('grp', 'tp')), may hold values from 0 to 2047, as said below
Outputs:
- attended: bfloat16 [2, 32768, 4096], P(None, ('grp', 'tp'))
Inputs may be any that keep to these rules, and one draw needn't show every extreme that they name: Inside each sequence of 2048 tokens positions count up by one and restart at 0 where a document begins; every sequence begins with 0, and the first sequence is one document.
All inputs are finite; a program needn't handle non-finite values.
Results may differ from a plain program's by a relative error of at most 0.011.
The roundings to bfloat16 on the way count: a program that leaves them out, or rounds other values in their place, can miss the bound.
Values may be sent and summed in bfloat16 or wider, within the bound.
No kernel may reach another device: no remote copies, remote signals or barrier semaphores. Data moves between devices by JAX's collectives and lax.ppermute only.
A program may use at most 192 MiB of HBM per device.

v0:
```python
import math

import jax
import jax.numpy as jnp
from jax import lax
from jax.sharding import PartitionSpec as P

HD = 128
QH = 32


rope_base = 500000.0


def rotate(values, positions):
    half = values.shape[-1] // 2
    freqs = rope_base ** (-jnp.arange(half, dtype=jnp.float32) * 2.0 / values.shape[-1])
    angles = positions.astype(jnp.float32)[:, None] * freqs[None, :]
    cosine = jnp.cos(angles)[:, None, :]
    sine = jnp.sin(angles)[:, None, :]
    first = values[..., :half]
    second = values[..., half:]
    return jnp.concatenate(
        [first * cosine - second * sine, second * cosine + first * sine], axis=-1
    )


def on_device(hidden, norm_gain, kv_weight, queries, positions):
    steps, rows, width = hidden.shape
    pair_cols = kv_weight.shape[1]
    half = pair_cols // 2
    heads_kv = half // HD
    groups = QH // heads_kv
    inv_root = 1.0 / math.sqrt(HD)
    wide = hidden.astype(jnp.float32)
    scale = lax.rsqrt(jnp.mean(wide * wide, axis=-1, keepdims=True) + 1e-05)
    normed = (wide * scale * norm_gain).astype(jnp.bfloat16).reshape(steps * rows, width)
    projected = jnp.dot(
        normed,
        lax.all_gather(kv_weight, ("grp", "tp"), axis=0, tiled=True),
        preferred_element_type=jnp.float32,
    )
    projected = projected.reshape(steps, rows, pair_cols)
    keys = jnp.stack(
        [
            rotate(projected[other, :, :half].reshape(rows, heads_kv, HD), positions)
            for other in range(steps)
        ]
    ).astype(jnp.bfloat16)
    values = projected[..., half:].reshape(steps, rows, heads_kv, HD).astype(jnp.bfloat16)
    local_queries = lax.all_to_all(queries, "tp", split_axis=1, concat_axis=2, tiled=True)
    rotated = jnp.stack(
        [rotate(local_queries[other].reshape(rows, QH, HD), positions) for other in range(steps)]
    ).astype(jnp.bfloat16)
    rotated = rotated.reshape(steps, rows, heads_kv, groups, HD)
    query_index = lax.axis_index("tp") * rows + jnp.arange(rows, dtype=jnp.int32)

    def attend(carry, piece, start):
        best, total, accum = carry
        key_piece = piece[0].reshape(-1, heads_kv, HD)
        value_piece = piece[1].reshape(-1, heads_kv, HD)
        count = key_piece.shape[0]
        scores = (
            jnp.einsum("sqhgd,khd->sqhgk", rotated, key_piece, preferred_element_type=jnp.float32)
            * inv_root
        )
        key_index = start + jnp.arange(count, dtype=jnp.int32)
        allowed = (key_index[None, :] <= query_index[:, None]) & (
            query_index[:, None] - key_index[None, :] <= positions[:, None]
        )
        allowed = allowed[None, :, None, None, :]
        scores = jnp.where(allowed, scores, -1e30)
        newbest = jnp.maximum(best, scores.max(-1))
        weights = jnp.where(allowed, jnp.exp(scores - newbest[..., None]), 0.0)
        factor = jnp.exp(best - newbest)
        total = total * factor + weights.sum(-1)
        accum = accum * factor[..., None] + jnp.einsum(
            "sqhgk,khd->sqhgd",
            weights.astype(jnp.bfloat16),
            value_piece,
            preferred_element_type=jnp.float32,
        )
        return (newbest, total, accum)

    initial = (
        jnp.full((steps, rows, heads_kv, groups), -1e30, jnp.float32),
        jnp.zeros((steps, rows, heads_kv, groups), jnp.float32),
        jnp.zeros((steps, rows, heads_kv, groups, HD), jnp.float32),
    )
    context_keys = keys[0].reshape(rows, half)
    context_values = values[0].reshape(rows, half)
    whole_keys, whole_values = (
        lax.all_gather(context_keys, "tp", axis=0, tiled=True),
        lax.all_gather(context_values, "tp", axis=0, tiled=True),
    )
    length = whole_keys.shape[0]
    block = min(512, length)

    def scan_block(bnumber, carry):
        start = (bnumber * block).astype(jnp.int32)
        piece = (
            lax.dynamic_slice_in_dim(whole_keys, start, block, 0),
            lax.dynamic_slice_in_dim(whole_values, start, block, 0),
        )
        return attend(carry, piece, start)

    best, total, accum = lax.fori_loop(0, length // block, scan_block, initial)
    results = []
    for step in range(steps):
        step_best = best[step]
        step_total = total[step]
        step_accum = accum[step]
        diagonal = [
            jnp.einsum(
                "qhgd,qhd->qhg", rotated[step], keys[other], preferred_element_type=jnp.float32
            )
            * inv_root
            for other in range(1, step + 1)
        ]
        merged = step_best
        for score in diagonal:
            merged = jnp.maximum(merged, score)
        factor = jnp.exp(step_best - merged)
        step_total = step_total * factor
        step_accum = step_accum * factor[..., None]
        for offset, score in enumerate(diagonal):
            weight = jnp.exp(score - merged)
            step_total = step_total + weight
            weight_round = weight.astype(jnp.bfloat16).astype(jnp.float32)
            step_accum = (
                step_accum
                + weight_round[..., None] * values[offset + 1].astype(jnp.float32)[:, :, None, :]
            )
        results.append(
            (step_accum / step_total[..., None]).astype(jnp.bfloat16).reshape(rows, QH * HD)
        )
    return jnp.stack(results)


def solution(mesh):
    placed = (
        P(None, ("grp", "tp"), None),
        P(),
        P(("grp", "tp"), None),
        P(None, "grp", "tp"),
        P(("grp", "tp")),
    )
    return jax.shard_map(
        on_device,
        mesh=mesh,
        in_specs=placed,
        out_specs=P(None, ("grp", "tp"), None),
        check_vma=False,
    )
```

profile of v0, /device:TPU:192, one launch (start us, length us, event | category | flops | bytes accessed | tf_op | source)
XLA Modules:
  0.0 1059.8 jit_solution(798990799239785391)
XLA Ops:
  7.3 3.1 fusion.17
  10.4 730.0 %all-gather.5.cloned.1.call-done = bf16[8192,1024]{1,0:T(8,128)(2,1)} async-done(((bf16[32,1024]{1,0:T(8,128)(2,1)}), bf16[8192,1024]{1,0:T(8,128)(2,1)}) %all-gather.5.cloned.1.call-update) | async-done | bytes 16777232 | tf_op jit(solution)/shard_map/all_gather | solution.py:40
  740.5 12.6 %fusion.37 = (bf16[2,128,1024]{2,1,0:T(8,128)(2,1)S(1)}, f32[2,128,1024]{2,1,0:T(8,128)}) fusion(bf16[8192,1024]{1,0:T(8,128)(2,1)} %all-gather.5.cloned.1.call-done, bf16[2,128,8192]{2,1,0:T(8,128)(2,1)} %param.7, f32[8192]{0:T(1024)S(1)} %copy-done.7, f32[2,128]{1,0:T(2,128)S(1)} %add_rsqrt_fusion), kind=kOutput, calls=%fused_computation.80 | convolution fusion | flops 4303618048 | bytes 22578176 | tf_op jit(solution)/shard_map/dot_general | solution.py:38
  753.9 14.0 %copy.58 = bf16[2,2048,256]{2,0,1:T(2,128)(2,1)} copy(bf16[2,2048,256]{2,1,0:T(8,128)(2,1)S(1)} %copy-done.3) | data formatting | bytes 4194304 | tf_op args[3]
  767.9 10.2 all-to-all-start
  782.2 48.9 %all-to-all-done = bf16[2,2048,256]{2,0,1:T(2,128)(2,1)S(1)} async-done(((bf16[2,2048,256]{2,0,1:T(2,128)(2,1)}), bf16[2,2048,256]{2,0,1:T(2,128)(2,1)S(1)}, u32[]{:S(2)}, u32[]{:S(2)}) %all-to-all-start) | async-done | bytes 2097184 | tf_op jit(solution)/shard_map/all_to_all | solution.py:51
  832.8 1.4 copy.62
  835.3 1.3 copy.63
  836.6 1.7 pad_maximum_fusion
  839.4 1.8 copy.88
  841.2 1.2 multiply_reduce_fusion
  842.4 17.0 %all-gather.9.cloned.1.call-done = bf16[1,2048,512]{2,1,0:T(8,128)(2,1)} async-done(((bf16[1,128,512]{2,1,0:T(8,128)(2,1)}), bf16[1,2048,512]{2,1,0:T(8,128)(2,1)}) %all-gather.9.cloned.1.call-update) | async-done | bytes 2097168 | tf_op jit(solution)/shard_map/all_gather | solution.py:94
  859.4 83.9 %all-gather.7.cloned.1.call-done = bf16[2048,512]{0,1:T(8,128)(2,1)} async-done(((bf16[128,512]{0,1:T(8,128)(2,1)}), bf16[2048,512]{0,1:T(8,128)(2,1)}) %all-gather.7.cloned.1.call-update) | async-done | bytes 2097168 | tf_op jit(solution)/shard_map/all_gather | solution.py:93
  943.3 66.9 %while.18 = (s32[]{:T(128)}, f32[2,128,4,8]{1,3,0,2:T(8,128)S(1)}, f32[2,128,4,8]{1,3,0,2:T(8,128)S(1)}, f32[2,128,4,8,128]{1,4,3,0,2:T(8,128)}, s32[128]{0:T(12...) while((s32[]{:T(128)}, f32[2,128,4,8]{1,3,0,2:T(8,128)S(1)}, ...), condition=%wide.region_4.5_spmd.clone, body=%wide.region_1.4_spmd.clone.sunk | while | flops 2205458944 | bytes 65806064 | solution.py:107
  943.4 1.1 constant_dynamic-slice_fusion.5
  944.8 1.1 constant_dynamic-slice_fusion.4
  945.8 2.6 fusion.56
  948.5 4.2 fusion.57
  952.8 6.1 bitcast_add_fusion.2
  959.0 1.1 constant_dynamic-slice_fusion.5
  960.3 1.1 constant_dynamic-slice_fusion.4
  961.4 2.6 fusion.56
  964.1 4.2 fusion.57
  968.3 7.6 bitcast_add_fusion.2
  977.4 1.1 constant_dynamic-slice_fusion.4
  978.5 2.6 fusion.56
  981.2 4.2 fusion.57
  985.5 7.6 bitcast_add_fusion.2
  994.6 1.1 constant_dynamic-slice_fusion.4
  995.7 2.6 fusion.56
  998.3 4.2 fusion.57
  1002.6 7.6 bitcast_add_fusion.2
  1010.2 4.8 fusion.34
  1015.0 1.9 copy.83
  1016.9 2.9 copy.84
  1021.3 2.6 broadcast_multiply_fusion
  1023.9 2.8 mul.330
  1026.6 1.9 mul.324
  1028.6 2.8 mul.325
  1031.4 1.9 div.55
  1033.3 2.7 div.56
  1036.0 1.9 mul.314
  1037.9 2.7 mul.315
  1040.7 1.9 div.52
  1042.6 2.8 div.53
  1045.4 2.8 divide_convert_fusion.1
  1049.5 2.2 divide_convert_fusion
  1051.7 1.5 pad_maximum_fusion.1
  (90 shorter events, 15.9 us)
Async XLA Ops:
  6.5 733.9 %copy-start.7 = (f32[8192]{0:T(1024)S(1)}, f32[8192]{0:T(1024)}, u32[]{:S(2)}) copy-start(f32[8192]{0:T(1024)} %param.8) | copy-start | bytes 98308
  6.5 733.9 %all-gather.5.cloned.1.call-start = ((), (), s32[]{:S(2)}) async-start(), calls=%async_computation.1 | async-start | bytes 16842752 | tf_op jit(solution)/shard_map/all_gather | solution.py:40
  7.3 852.2 %all-gather.9.cloned.1.call-start = ((), (), s32[]{:S(2)}) async-start(), calls=%async_computation.3 | async-start | bytes 2228224 | tf_op jit(solution)/shard_map/all_gather | solution.py:94
  10.4 743.4 %copy-start.3 = (bf16[2,2048,256]{2,1,0:T(8,128)(2,1)S(1)}, bf16[2,2048,256]{2,1,0:T(8,128)(2,1)}, u32[]{:S(2)}) copy-start(bf16[2,2048,256]{2,1,0:T(8,128)(2,1)} %param.10) | copy-start | bytes 6291460
  753.9 24.3 %copy-start.4 = (s32[128]{0:T(128)S(1)}, s32[128]{0:T(128)}, u32[]{:S(2)}) copy-start(s32[128]{0:T(128)} %param.11) | copy-start | bytes 1540
  767.9 63.2 %all-to-all-start = ((bf16[2,2048,256]{2,0,1:T(2,128)(2,1)}), bf16[2,2048,256]{2,0,1:T(2,128)(2,1)S(1)}, u32[]{:S(2)}, u32[]{:S(2)}) async-start(bf16[2,2048,256]{2,0,1:T(2,128)(2,1)} %copy.58), calls=%async_computation | async-start | bytes 4194304 | tf_op jit(solution)/shard_map/all_to_all | solution.py:51
  778.1 165.2 %all-gather.7.cloned.1.call-start = ((), (), s32[]{:S(2)}) async-start(), calls=%async_computation.2 | async-start | bytes 2228224 | tf_op jit(solution)/shard_map/all_gather | solution.py:93
  835.3 108.0 %copy-start.5 = (s32[128]{0:T(128)S(1)}, s32[128]{0:T(128)}, u32[]{:S(2)}) copy-start(s32[128]{0:T(128)} %param.11) | copy-start | bytes 1540
  952.8 6.1 copy-start.6
  968.3 7.7 copy-start.6
  985.4 7.7 copy-start.6
  1002.6 7.7 copy-start.6
  1045.4 2.9 copy-start
  1045.4 3.5 copy-start.1
  1045.4 4.1 copy-start.2
Sparse Core Ops, SparseCore 0:
  9.2 731.1 all-gather.4
  754.0 105.3 all-gather.8
  861.9 81.3 all-gather.6
where the time goes:
time: 1060 us
  waiting for transfers between devices  881 us (83%)
  local copies, waits for them, and re-layouts  67.1 us (6%)
  matrix products  52.1 us (5%)
  other arithmetic  36.1 us (3%)
  between operations  13.4 us (1%)
    all_gather x1, waiting for transfers between devices, on_device(): lax.all_gather(kv_weight, ('grp', 'tp'), axis=0, tiled=True)  730 us
    all_gather x1, waiting for transfers between devices, on_device(): lax.all_gather(context_keys, 'tp', axis=0, tiled=True)  83.9 us
    all_to_all x1, waiting for transfers between devices, on_device(): lax.all_to_all(queries, 'tp', split_axis=1, concat_axis=2, tiled=True)  48.9 us
    dot_general x4, matrix products, attend(): jnp.einsum('sqhgk,khd->sqhgd', weights.astype(jnp.bfloat16), value_piece,...  29 us
  transfers between devices with their start and end apart: 4, of which 4 were waited for; matrix products, arithmetic and copies ran while one was open for 3% of the time, Pallas kernels for 0%

commit v1 on v0

v1 whole, which is shorter than its diff:
```python
import math

import jax
import jax.numpy as jnp
from jax import lax
from jax.experimental import pallas as pl
from jax.experimental.pallas import tpu as pltpu
from jax.sharding import PartitionSpec as P

HD = 128
QH = 32
KVH = 4
BOTH = ("grp", "tp")
COLS_A = 640
SLOTS_Z = (0, -1, 1, -2, 2, -3, 3, -4)
SLOTS_4 = (0, -1, 1, -2)
BLOCK = 512
TILE = 512
VMEM = 56 * 1024 * 1024
NEG = -1e30
rope_base = 500000.0


def coords(grp, tp):
    return grp // 4, (tp % 2) * 2 + (grp // 2) % 2, tp // 2, grp % 2


def place(x, y, z, core):
    return ((x * 2 + y % 2) * 2 + core) * 16 + z * 2 + y // 2


def shift(value, dx=0, dy=0, dz=0, swap=False):
    pairs = []
    for device in range(256):
        x, y, z, core = coords(device // 16, device % 16)
        target = place((x + dx) % 4, (y + dy) % 4, (z + dz) % 8, 1 - core if swap else core)
        pairs.append((device, target))
    return lax.ppermute(value, BOTH, pairs)


def ring8(block):
    up, down = shift(block, dz=1), shift(block, dz=-1)
    found = [block, up, down]
    for _ in range(2):
        up, down = shift(up, dz=1), shift(down, dz=-1)
        found += [up, down]
    found.append(shift(up, dz=1))
    return found


def ring4(block, axis):
    half = block.shape[0] // 2
    up, down = shift(block, **{axis: 1}), shift(block, **{axis: -1})
    far = shift(up[:half], **{axis: 1}), shift(down[half:], **{axis: -1})
    return [block, up, down, far[0], far[1]]


def norm_body(core_ref, hidden_ref, gain_ref, mine_ref, other_ref):
    core = core_ref[0]
    wide = hidden_ref[...].astype(jnp.float32)
    scale = lax.rsqrt(jnp.mean(wide * wide, axis=-1, keepdims=True) + 1e-05)
    for group in range(8):
        for out_ref, which in ((mine_ref, core), (other_ref, 1 - core)):
            start = pl.multiple_of((2 * group + which) * 512, 512)
            part = hidden_ref[:, pl.ds(start, 512)].astype(jnp.float32)
            gain = gain_ref[:, pl.ds(start, 512)]
            out_ref[:, group * 512 : (group + 1) * 512] = (part * scale * gain).astype(jnp.bfloat16)


def norm(hidden, gain, core):
    rows, width = hidden.shape
    out = jax.ShapeDtypeStruct((rows, width // 2), jnp.bfloat16)
    return pl.pallas_call(
        norm_body,
        out_shape=(out, out),
        grid=(rows // 64,),
        in_specs=[
            pl.BlockSpec(memory_space=pltpu.SMEM),
            pl.BlockSpec((64, width), lambda i: (i, 0)),
            pl.BlockSpec((1, width), lambda i: (0, 0)),
        ],
        out_specs=(
            pl.BlockSpec((64, width // 2), lambda i: (i, 0)),
            pl.BlockSpec((64, width // 2), lambda i: (i, 0)),
        ),
        compiler_params=pltpu.CompilerParams(vmem_limit_bytes=VMEM),
        name="norm",
    )(core, hidden, gain)


def project_body(where_ref, mine_ref, other_ref, *refs):
    a_refs, b_refs = refs[0:5], refs[5:10]
    out_ref, weight = refs[10], refs[11]
    x0, y0, z0 = where_ref[0], where_ref[1], where_ref[2]
    last = ((0, 0, 4), (-1, 0, 4), (1, 0, 4), (-2, 0, 2), (-2, 2, 2))

    def rel(slot):
        step = (slot + 1) // 2
        return jnp.where(slot % 2 == 1, -step, step)

    for which, group in ((0, a_refs), (1, b_refs)):
        for ref, (off, first, count) in zip(group, last):
            lo, hi = (0, COLS_A) if which == 0 else (COLS_A, weight.shape[1])

            def copy(index, _, ref=ref, off=off, first=first, which=which, lo=lo, hi=hi):
                mid, zslot = index // 8, index % 8
                other = rel(mid + first)
                x = (x0 + (off if which == 0 else other) + 4) % 4
                y = (y0 + (other if which == 0 else off) + 4) % 4
                z = (z0 + rel(zslot) + 8) % 8
                row = (x * 2 + y % 2) * 512 + z * 64 + (y // 2) * 32
                weight[pl.ds(pl.multiple_of(row, 32), 32), lo:hi] = ref[mid, zslot]
                return 0

            lax.fori_loop(0, count * 8, copy, 0)
    rows = mine_ref.shape[0]
    for index, ref in enumerate((mine_ref, other_ref)):
        out_ref[index * rows : (index + 1) * rows, :] = jnp.dot(
            ref[...], weight[...], preferred_element_type=jnp.float32
        )


def project(where, mine, other, pieces_a, pieces_b):
    rows, depth = mine.shape
    cols = pieces_a[0].shape[-1] + pieces_b[0].shape[-1]
    vmem = pl.BlockSpec(memory_space=pltpu.VMEM)
    return pl.pallas_call(
        project_body,
        out_shape=jax.ShapeDtypeStruct((2 * rows, cols), jnp.float32),
        in_specs=[pl.BlockSpec(memory_space=pltpu.SMEM)] + [vmem] * 12,
        out_specs=vmem,
        scratch_shapes=[pltpu.VMEM((depth, cols), jnp.bfloat16)],
        compiler_params=pltpu.CompilerParams(vmem_limit_bytes=VMEM),
        name="project",
    )(where, mine, other, *pieces_a, *pieces_b)


def turn(values, cosine, sine):
    return values * cosine + pltpu.roll(values, 64, 1) * sine


def keys_values_body(own_ref, got_ref, cos_ref, sin_ref, first_ref, second_ref):
    rows = first_ref.shape[0]
    cosine, sine = cos_ref[...], sin_ref[...]
    for step, out_ref in enumerate((first_ref, second_ref)):
        for head in range(2 * KVH):
            cols = slice(head * HD, (head + 1) * HD)
            part = own_ref[step * rows : (step + 1) * rows, cols]
            part = part + got_ref[step * rows : (step + 1) * rows, cols]
            if head < KVH:
                part = turn(part, cosine, sine)
            out_ref[:, cols] = part.astype(jnp.bfloat16)


def keys_values(own, got, cosine, sine):
    rows, cols = own.shape
    out = jax.ShapeDtypeStruct((rows // 2, cols), jnp.bfloat16)
    vmem = pl.BlockSpec(memory_space=pltpu.VMEM)
    return pl.pallas_call(
        keys_values_body,
        out_shape=(out, out),
        in_specs=[vmem] * 4,
        out_specs=(vmem, vmem),
        compiler_params=pltpu.CompilerParams(vmem_limit_bytes=VMEM),
        name="keys_values",
    )(own, got, cosine, sine)


def attend_body(info_ref, q_ref, cos_ref, sin_ref, low_ref, k1_ref, v1_ref, *refs):
    k_refs, v_refs = refs[0:8], refs[8:16]
    out_ref, keys, values, scores, maxima, rotated = refs[16:]
    z0, first, low_first, low_last = info_ref[0], info_ref[1], info_ref[2], info_ref[3]
    rows = low_ref.shape[0]
    inv_root = 1.0 / math.sqrt(HD)
    to_two = inv_root * math.log2(math.e)

    for off, k_ref, v_ref in zip(SLOTS_Z, k_refs, v_refs):
        start = pl.multiple_of(((z0 + off + 8) % 8) * 256, 256)
        keys[pl.ds(start, 256), :] = k_ref[...]
        values[pl.ds(start, 256), :HD] = v_ref[...]
    values[:, HD:] = jnp.ones((values.shape[0], HD), jnp.bfloat16)

    cosine, sine = cos_ref[...], sin_ref[...]
    begin = low_first // BLOCK
    end = (first + rows - 1) // BLOCK + 1
    token = first + lax.broadcasted_iota(jnp.int32, (rows, BLOCK), 0)
    low = low_ref[...]

    def tile(source, _):
        for step in range(2):
            for half in range(2):
                at = (step * 2 + half) * rows
                value = q_ref[source, step, :, half * HD : (half + 1) * HD].astype(jnp.float32)
                rotated[at : at + rows, :] = turn(value, cosine, sine).astype(jnp.bfloat16)
        maxima[...] = jnp.full(maxima.shape, NEG, jnp.float32)

        def score(block, _):
            start = pl.multiple_of(block * BLOCK, BLOCK)
            found = lax.dot_general(
                rotated[...],
                keys[pl.ds(start, BLOCK), :],
                (((1,), (1,)), ((), ())),
                preferred_element_type=jnp.float32,
            )
            whole = (start >= low_last) & (start + BLOCK - 1 <= first)

            @pl.when(whole)
            def _():
                scores[block] = found
                best = maxima[...]
                for part in range(BLOCK // HD):
                    best = jnp.maximum(best, found[:, part * HD : (part + 1) * HD])
                maxima[...] = best

            @pl.when(jnp.logical_not(whole))
            def _():
                key = start + lax.broadcasted_iota(jnp.int32, (rows, BLOCK), 1)
                allowed = (key <= token) & (key >= low)
                for index in range(4):
                    at = slice(index * rows, (index + 1) * rows)
                    masked = jnp.where(allowed, found[at, :], NEG)
                    scores[block, at, :] = masked
                    best = maxima[at, :]
                    for part in range(BLOCK // HD):
                        best = jnp.maximum(best, masked[:, part * HD : (part + 1) * HD])
                    maxima[at, :] = best

            return 0

        lax.fori_loop(begin, end, score, 0)
        best = jnp.max(maxima[...], axis=1, keepdims=True)
        k1 = k1_ref[...].astype(jnp.float32)
        diagonal = jnp.sum(
            rotated[2 * rows :, :].astype(jnp.float32).reshape(2, rows, HD) * k1[None], axis=-1, keepdims=True
        ).reshape(2 * rows, 1)
        best = jnp.concatenate([best[: 2 * rows], jnp.maximum(best[2 * rows :], diagonal)], axis=0)
        shifted = best * to_two

        def weigh(block, total):
            start = pl.multiple_of(block * BLOCK, BLOCK)
            weights = jnp.exp2(scores[block] * to_two - shifted).astype(jnp.bfloat16)
            return total + jnp.dot(weights, values[pl.ds(start, BLOCK), :], preferred_element_type=jnp.float32)

        total = lax.fori_loop(begin, end, weigh, jnp.zeros((4 * rows, 2 * HD), jnp.float32))
        accum, count = total[:, :HD], total[:, HD:]
        own = jnp.exp2(diagonal * to_two - shifted[2 * rows :])
        v1 = v1_ref[...].astype(jnp.float32)
        own_round = own.astype(jnp.bfloat16).astype(jnp.float32)
        extra = (own_round.reshape(2, rows, 1) * v1[None]).reshape(2 * rows, HD)
        for step in range(2):
            for half in range(2):
                index = step * 2 + half
                at = slice(index * rows, (index + 1) * rows)
                top, below = accum[at], count[at]
                if step == 1:
                    here = slice(half * rows, (half + 1) * rows)
                    top, below = top + extra[here], below + own[here]
                column = pl.multiple_of(source * 2 * HD, 2 * HD) + half * HD
                out_ref[step, :, pl.ds(column, HD)] = (top / below).astype(jnp.bfloat16)
        return 0

    lax.fori_loop(0, 4, tile, 0)


def attend(info, queries, cosine, sine, low, kv1, blocks):
    rows = low.shape[0]
    whole = lambda h: (0, 0)
    key_col = lambda h: (0, h)
    value_col = lambda h: (0, KVH + h)
    length = 256 * len(blocks)
    return pl.pallas_call(
        attend_body,
        out_shape=jax.ShapeDtypeStruct((2, rows, QH * HD), jnp.bfloat16),
        grid=(KVH,),
        in_specs=[
            pl.BlockSpec(memory_space=pltpu.SMEM),
            pl.BlockSpec((4, 2, rows, 2 * HD), lambda h: (h, 0, 0, 0)),
            pl.BlockSpec((rows, HD), whole),
            pl.BlockSpec((rows, HD), whole),
            pl.BlockSpec((rows, 1), whole),
            pl.BlockSpec((rows, HD), key_col),
            pl.BlockSpec((rows, HD), value_col),
        ]
        + [pl.BlockSpec((256, HD), key_col)] * 8
        + [pl.BlockSpec((256, HD), value_col)] * 8,
        out_specs=pl.BlockSpec((2, rows, 8 * HD), lambda h: (0, 0, h)),
        scratch_shapes=[
            pltpu.VMEM((length, HD), jnp.bfloat16),
            pltpu.VMEM((length, 2 * HD), jnp.bfloat16),
            pltpu.VMEM((length // BLOCK, 4 * rows, BLOCK), jnp.float32),
            pltpu.VMEM((4 * rows, HD), jnp.float32),
            pltpu.VMEM((4 * rows, HD), jnp.bfloat16),
        ],
        compiler_params=pltpu.CompilerParams(vmem_limit_bytes=VMEM),
        name="attend",
    )(info, queries, cosine, sine, low, kv1, kv1, *blocks, *blocks)


def on_device(hidden, norm_gain, kv_weight, queries, positions):
    steps, rows, width = hidden.shape
    grp, tp = lax.axis_index("grp"), lax.axis_index("tp")
    x, y, z, core = coords(grp, tp)
    where = jnp.stack([x, y, z, core]).astype(jnp.int32)

    sent = queries.reshape(steps, 16, rows, 2 * HD).transpose(1, 0, 2, 3)
    local_queries = lax.all_to_all(sent, "tp", split_axis=0, concat_axis=0, tiled=True)

    along = jnp.stack(ring8(kv_weight))
    first_a = ring4(along[:, :, :COLS_A], "dy")
    first_b = ring4(along[:, :, COLS_A:], "dx")

    def joined(found):
        return jnp.stack([found[0], found[1], found[2], jnp.concatenate([found[3], found[4]])])

    pieces_a = ring4(joined(first_a), "dx")
    pieces_b = ring4(joined(first_b), "dy")

    mine, other = norm(hidden.reshape(steps * rows, width), norm_gain[None, :], where[3:])
    other = shift(other, swap=True)

    freqs = rope_base ** (-jnp.arange(HD // 2, dtype=jnp.float32) * 2.0 / HD)
    angles = positions.astype(jnp.float32)[:, None] * freqs[None, :]
    cosine, sine = jnp.cos(angles), jnp.sin(angles)
    cosine = jnp.concatenate([cosine, cosine], axis=-1)
    sine = jnp.concatenate([-sine, sine], axis=-1)

    projected = project(where[:3], mine, other, pieces_a, pieces_b)
    got = shift(projected[steps * rows :], swap=True)
    kv0, kv1 = keys_values(projected[: steps * rows], got, cosine, sine)

    partner = shift(kv0, dy=2)
    pair = jnp.where(tp % 2 == 0, jnp.concatenate([kv0, partner]), jnp.concatenate([partner, kv0]))
    blocks = ring8(pair)

    first = (tp * rows).astype(jnp.int32)
    low = first + jnp.arange(rows, dtype=jnp.int32) - positions
    info = jnp.stack([z.astype(jnp.int32), first, low[0], low[rows - 1]])
    return attend(info, local_queries, cosine, sine, low[:, None], kv1, blocks)


def solution(mesh):
    placed = (
        P(None, ("grp", "tp"), None),
        P(),
        P(("grp", "tp"), None),
        P(None, "grp", "tp"),
        P(("grp", "tp")),
    )
    return jax.shard_map(
        on_device,
        mesh=mesh,
        in_specs=placed,
        out_specs=P(None, ("grp", "tp"), None),
        check_vma=False,
    )
```

time: 1060 us -> 288 us (0.27)
  waiting for transfers between devices: 881 us -> 119 us
  Pallas kernels: 0 us -> 94.6 us
  local copies, waits for them, and re-layouts: 67.1 us -> 11.7 us
  matrix products: 52.1 us -> 0 us
  starting transfers between devices: 10.3 us -> 56.3 us
  other arithmetic: 36.1 us -> 5.25 us
  between operations: 13.4 us -> 0.42 us
    all_gather x3 -> x0, waiting for transfers between devices: 831 us -> none  [the longest x1 730 us: on_device(): lax.all_gather(kv_weight, ('grp', 'tp'), axis=0, tiled=True)]
    ppermute x0 -> x33, waiting for transfers between devices: none -> 119 us  [shift(): return lax.ppermute(value, BOTH, pairs)]
    pallas_call x0 -> x4, Pallas kernels: none -> 94.6 us  [the longest x1 65.3 us: attend(): pl.pallas_call(attend_body, out_shape=jax.ShapeDtypeStruct((2, rows, QH *...]
    dot_general x9 -> x0, matrix products: 52.1 us -> none  [the longest x4 29 us: attend(): jnp.einsum('sqhgk,khd->sqhgd', weights.astype(jnp.bfloat16), value_piece,...]
    all_to_all x1, waiting for transfers between devices: 48.9 us -> 0.01 us  [on_device(): lax.all_to_all(sent, 'tp', split_axis=0, concat_axis=0, tiled=True)]
    ppermute x0 -> x33, starting transfers between devices: none -> 45.1 us  [shift(): return lax.ppermute(value, BOTH, pairs)]
    reduce_sum x5 -> x0, other arithmetic: 20 us -> none  [the longest x4 16.9 us: attend(): total = total * factor + weights.sum(-1)]
    unnamed x16 -> x37, local copies, waits for them, and re-layouts: 17.1 us -> 2.76 us
  transfers between devices with their start and end apart: 4 -> 34, of which waited for: 4 -> 18; matrix products, arithmetic and copies ran while one was open for 3% -> 5% of each run, Pallas kernels for 0% -> 10%
where the time goes in v1:
time: 288 us; the launch traced here: 287 us
  waiting for transfers between devices  119 us (41%)
  Pallas kernels  94.6 us (33%)
  starting transfers between devices  56.3 us (20%)
  local copies, waits for them, and re-layouts  11.7 us (4%)
  other arithmetic  5.25 us (2%)
    ppermute x33, waiting for transfers between devices, shift(): return lax.ppermute(value, BOTH, pairs)  119 us
    pallas_call x1, Pallas kernels, attend(): pl.pallas_call(attend_body, out_shape=jax.ShapeDtypeStruct((2, rows, QH *...  65.3 us
    ppermute x33, starting transfers between devices, shift(): return lax.ppermute(value, BOTH, pairs)  45.1 us
    pallas_call x1, Pallas kernels, project(): pl.pallas_call(project_body, out_shape=jax.ShapeDtypeStruct((2 * rows, co...  21.1 us
    all_to_all x1, starting transfers between devices, on_device(): lax.all_to_all(sent, 'tp', split_axis=0, concat_axis=0, tiled=True)  11.2 us
  transfers between devices with their start and end apart: 34, of which 18 were waited for; matrix products, arithmetic and copies ran while one was open for 5% of the time, Pallas kernels for 10%

profile of v1, /device:TPU:192, one launch (start us, length us, event | category | flops | bytes accessed | tf_op | source)
XLA Modules:
  0.0 287.3 jit_solution(16669098604637941435)
XLA Ops:
  0.0 1.0 collective-permute-start.1
  1.0 1.0 collective-permute-start.2
  2.9 1.6 collective-permute-done.1
  4.5 1.0 collective-permute-start.3
  5.5 1.1 collective-permute-start.4
  6.6 2.1 collective-permute-done.3
  8.7 1.0 collective-permute-start.5
  9.9 1.0 collective-permute-start.6
  10.9 2.3 collective-permute-done.5
  13.1 1.3 collective-permute-start.7
  14.5 3.1 %collective-permute-done.7 = bf16[32,1024]{1,0:T(8,128)(2,1)S(1)} collective-permute-done((bf16[32,1024]{1,0:T(8,128)(2,1)S(1)}, bf16[32,1024]{1,0:T(8,128)(2,1)S(1)}, u32[]{:S(2)}, u32[]{:S(2)}) %collective-permute-start.7) | collective-permute-done | bytes 65568 | tf_op jit(solution)/shard_map/ppermute | solution.py:38
  17.7 1.7 collective-permute-start.8
  19.4 1.7 collective-permute-start.9
  21.0 6.3 %collective-permute-done.8 = bf16[8,32,640]{2,1,0:T(8,128)(2,1)S(1)} collective-permute-done((bf16[8,32,640]{2,1,0:T(8,128)(2,1)S(1)}, bf16[8,32,640]{2,1,0:T(8,128)(2,1)S(1)}, u32[]{:S(2)}, u32[]{:S(2)}) %collective-permute-start.8) | collective-permute-done | bytes 327712 | tf_op jit(solution)/shard_map/ppermute | solution.py:38
  27.4 0.9 collective-permute-start.10
  28.3 2.5 collective-permute-start.11
  30.9 5.6 %norm.1 = (bf16[256,4096]{1,0:T(8,128)(2,1)}, bf16[256,4096]{1,0:T(8,128)(2,1)}) custom-call(s32[1]{0:T(128)} %bitcast.7.core_ref, bf16[256,8192]{1,0:T(8,128)(2,1)} %bitcast.41, f32[1,8192]{1,0:T(1,128)} %bitcast.47), custom_call_target="tpu_custom_call" | custom-call | tf_op jit(solution)/shard_map/norm/pallas_call | solution.py:73
  36.8 1.6 collective-permute-start.12
  38.4 1.7 collective-permute-start.13
  40.7 3.0 %collective-permute-start.17 = (bf16[8,32,384]{2,1,0:T(8,128)(2,1)S(1)}, bf16[8,32,384]{2,1,0:T(8,128)(2,1)S(1)}, u32[]{:S(2)}, u32[]{:S(2)}) collective-permute-start(bf16[8,32,384]{2,1,0:T(8,128)(2,1)S(1)} %get-tuple-element.16), channel_id=1, source_target_pairs={{0,192},{1,193},{2,194},{3,195},{4,196},{5,197},{6,198},{7,199},{8... | collective-permute-start | bytes 589832 | tf_op jit(solution)/shard_map/ppermute | solution.py:38
  43.6 29.8 %collective-permute-done.16 = bf16[8,32,384]{2,1,0:T(8,128)(2,1)S(1)} collective-permute-done((bf16[8,32,384]{2,1,0:T(8,128)(2,1)S(1)}, bf16[8,32,384]{2,1,0:T(8,128)(2,1)S(1)}, u32[]{:S(2)}, u32[]{:S(2)}) %collective-permute-start.16) | collective-permute-done | bytes 196640 | tf_op jit(solution)/shard_map/ppermute | solution.py:38
  73.8 3.0 %collective-permute-start.19 = (bf16[4,32,384]{2,1,0:T(8,128)(2,1)S(1)}, bf16[4,32,384]{2,1,0:T(8,128)(2,1)S(1)}, u32[]{:S(2)}, u32[]{:S(2)}) collective-permute-start(bf16[4,32,384]{2,1,0:T(8,128)(2,1)S(1)} %slice.63), channel_id=1, source_target_pairs={{0,192},{1,193},{2,194},{3,195},{4,196},{5,197},{6,198},{7,199},{8... | collective-permute-start | bytes 294920 | tf_op jit(solution)/shard_map/ppermute | solution.py:38
  76.9 2.5 collective-permute-done.18
  79.7 3.2 %collective-permute-start.21 = (bf16[4,8,32,384]{3,2,1,0:T(8,128)(2,1)S(1)}, bf16[4,8,32,384]{3,2,1,0:T(8,128)(2,1)S(1)}, u32[]{:S(2)}, u32[]{:S(2)}) collective-permute-start(bf16[4,8,32,384]{3,2,1,0:T(8,128)(2,1)S(1)} %pad_maximum_fusion.1.refs_5_), channel_id=1, source_target_pairs={{0,33},{1,32},{2,35},{3,34},{4,37},{5,36},{6,39},{7,38},{8,41},{9,... | collective-permute-start | bytes 2359304 | tf_op jit(solution)/shard_map/ppermute | solution.py:38
  82.9 1.0 slice.59
  84.6 2.8 collective-permute-start.15
  87.4 11.5 %collective-permute-done.20.refs_6_ = bf16[4,8,32,384]{3,2,1,0:T(8,128)(2,1)S(1)} collective-permute-done((bf16[4,8,32,384]{3,2,1,0:T(8,128)(2,1)S(1)}, bf16[4,8,32,384]{3,2,1,0:T(8,128)(2,1)S(1)}, u32[]{:S(2)}, u32[]{:S(2)}) %collective-permute-start.20) | collective-permute-done | bytes 786464 | tf_op jit(solution)/shard_map/ppermute | solution.py:38
  100.7 3.2 %collective-permute-start.23 = (bf16[2,8,32,384]{3,2,1,0:T(8,128)(2,1)}, bf16[2,8,32,384]{3,2,1,0:T(8,128)(2,1)}, u32[]{:S(2)}, u32[]{:S(2)}) collective-permute-start(bf16[2,8,32,384]{3,2,1,0:T(8,128)(2,1)} %slice.65), channel_id=1, source_target_pairs={{0,33},{1,32},{2,35},{3,34},{4,37},{5,36},{6,39},{7,38},{8,41},{9,... | collective-permute-start | bytes 1179656 | tf_op jit(solution)/shard_map/ppermute | solution.py:38
  103.9 1.5 copy.10
  105.4 11.2 %all-to-all-start = ((bf16[16,2,128,256]{3,2,1,0:T(8,128)(2,1)}), bf16[16,2,128,256]{3,2,1,0:T(8,128)(2,1)S(1)}, u32[]{:S(2)}, u32[]{:S(2)}) async-start(bf16[16,2,128,256]{3,2,1,0:T(8,128)(2,1)} %bitcast.40), calls=%async_computation | async-start | bytes 4194304 | tf_op jit(solution)/shard_map/all_to_all | solution.py:306
  118.0 21.1 %project.1 = f32[512,1024]{1,0:T(8,128)} custom-call(s32[3]{0:T(128)} %pad_add_fusion.1.where_ref, bf16[256,4096]{1,0:T(8,128)(2,1)} %get-tuple-element.9.mine_ref, bf16[256,4096]{1,0:T(8,128)(2,1)} %collective-permute-done.other_ref, bf16[4,8,32,640]{3,2,1,0:T(8,128)(2,1)} %copy-done.1, bf16[4,8,32,640]{3,2,1,0:T(8,128)(2,1)} %copy-done.4, ...), custom_call_target="tpu_custom_call" | custom-call | tf_op jit(solution)/shard_map/project/pallas_call | solution.py:127
  139.1 3.2 %fusion.1 = (f32[256,1024]{1,0:T(8,128)}, f32[256,1024]{1,0:T(8,128)}) fusion(f32[512,1024]{1,0:T(8,128)} %project.1), kind=kLoop, calls=%fused_computation.25 | loop fusion | bytes 4194304 | tf_op jit(solution)/shard_map/slice | solution.py:328
  143.4 1.8 collective-permute-done.24.got_ref
  145.2 1.0 copy-done.12
  146.2 2.5 keys_values.1
  148.7 3.0 %collective-permute-start.25 = (bf16[128,1024]{1,0:T(8,128)(2,1)}, bf16[128,1024]{1,0:T(8,128)(2,1)S(1)}, u32[]{:S(2)}, u32[]{:S(2)}) collective-permute-start(bf16[128,1024]{1,0:T(8,128)(2,1)} %get-tuple-element.12), channel_id=1, source_target_pairs={{0,1},{1,0},{2,3},{3,2},{4,5},{5,4},{6,7},{7,6},{8,9},{9,8},{10,11... | collective-permute-start | bytes 786440 | tf_op jit(solution)/shard_map/ppermute | solution.py:38
  151.7 16.4 %collective-permute-done.25 = bf16[128,1024]{1,0:T(8,128)(2,1)S(1)} collective-permute-done((bf16[128,1024]{1,0:T(8,128)(2,1)}, bf16[128,1024]{1,0:T(8,128)(2,1)S(1)}, u32[]{:S(2)}, u32[]{:S(2)}) %collective-permute-start.25) | collective-permute-done | bytes 262176 | tf_op jit(solution)/shard_map/ppermute | solution.py:38
  168.1 1.2 maximum_select_fusion.refs_0_.refs_8_
  169.4 2.0 collective-permute-start.27
  171.4 11.6 %collective-permute-done.26.refs_1_.refs_9_ = bf16[256,1024]{1,0:T(8,128)(2,1)S(1)} collective-permute-done((bf16[256,1024]{1,0:T(8,128)(2,1)S(1)}, bf16[256,1024]{1,0:T(8,128)(2,1)S(1)}, u32[]{:S(2)}, u32[]{:S(2)}) %collective-permute-start.26) | collective-permute-done | bytes 524320 | tf_op jit(solution)/shard_map/ppermute | solution.py:38
  183.4 1.6 collective-permute-start.29
  185.0 10.7 %collective-permute-done.28.refs_3_.refs_11_ = bf16[256,1024]{1,0:T(8,128)(2,1)S(1)} collective-permute-done((bf16[256,1024]{1,0:T(8,128)(2,1)S(1)}, bf16[256,1024]{1,0:T(8,128)(2,1)S(1)}, u32[]{:S(2)}, u32[]{:S(2)}) %collective-permute-start.28) | collective-permute-done | bytes 524320 | tf_op jit(solution)/shard_map/ppermute | solution.py:38
  195.8 1.2 collective-permute-start.30
  197.6 1.6 collective-permute-start.31
  199.2 10.0 %collective-permute-done.30.refs_5_.refs_13_ = bf16[256,1024]{1,0:T(8,128)(2,1)} collective-permute-done((bf16[256,1024]{1,0:T(8,128)(2,1)S(1)}, bf16[256,1024]{1,0:T(8,128)(2,1)}, u32[]{:S(2)}, u32[]{:S(2)}) %collective-permute-start.30) | collective-permute-done | bytes 524320 | tf_op jit(solution)/shard_map/ppermute | solution.py:38
  211.5 2.0 pad_add_fusion.info_ref
  213.5 8.3 %collective-permute-done.32.refs_7_.refs_15_ = bf16[256,1024]{1,0:T(8,128)(2,1)} collective-permute-done((bf16[256,1024]{1,0:T(8,128)(2,1)}, bf16[256,1024]{1,0:T(8,128)(2,1)}, u32[]{:S(2)}, u32[]{:S(2)}) %collective-permute-start.32) | collective-permute-done | bytes 524320 | tf_op jit(solution)/shard_map/ppermute | solution.py:38
  221.8 65.3 %attend.1 = bf16[2,128,4096]{2,1,0:T(8,128)(2,1)} custom-call(s32[4]{0:T(128)} %pad_add_fusion.info_ref, bf16[16,2,128,256]{3,2,1,0:T(8,128)(2,1)} %copy-done, f32[128,128]{1,0:T(8,128)} %get-tuple-element.26.cos_ref, f32[128,128]{1,0:T(8,128)} %get-tuple-element.27.sin_ref, s32[128,1]{1,0:T(8,128)} %copy.8.low_ref, ...), custom_call_target="tpu_custom_call" | custom-call | tf_op jit(solution)/shard_map/attend/pallas_call | solution.py:271
  (87 shorter events, 11.0 us)
Async XLA Ops:
  0.0 4.5 %collective-permute-start.1 = (bf16[32,1024]{1,0:T(8,128)(2,1)}, bf16[32,1024]{1,0:T(8,128)(2,1)S(1)}, u32[]{:S(2)}, u32[]{:S(2)}) collective-permute-start(bf16[32,1024]{1,0:T(8,128)(2,1)} %param.7), channel_id=1, source_target_pairs={{0,2},{1,3},{2,4},{3,5},{4,6},{5,7},{6,8},{7,9},{8,10},{9,11},{10,... | collective-permute-start | bytes 196616 | tf_op jit(solution)/shard_map/ppermute | solution.py:38
  1.0 4.5 %collective-permute-start.2 = (bf16[32,1024]{1,0:T(8,128)(2,1)}, bf16[32,1024]{1,0:T(8,128)(2,1)S(1)}, u32[]{:S(2)}, u32[]{:S(2)}) collective-permute-start(bf16[32,1024]{1,0:T(8,128)(2,1)} %param.7), channel_id=1, source_target_pairs={{0,14},{1,15},{2,0},{3,1},{4,2},{5,3},{6,4},{7,5},{8,6},{9,7},{10,... | collective-permute-start | bytes 196616 | tf_op jit(solution)/shard_map/ppermute | solution.py:38
  4.5 4.3 %collective-permute-start.3 = (bf16[32,1024]{1,0:T(8,128)(2,1)S(1)}, bf16[32,1024]{1,0:T(8,128)(2,1)S(1)}, u32[]{:S(2)}, u32[]{:S(2)}) collective-permute-start(bf16[32,1024]{1,0:T(8,128)(2,1)S(1)} %collective-permute-done.1), channel_id=1, source_target_pairs={{0,2},{1,3},{2,4},{3,5},{4,6},{5,7},{6,8},{7,9},{8,10},{9,11},{10,... | collective-permute-start | bytes 196616 | tf_op jit(solution)/shard_map/ppermute | solution.py:38
  5.5 4.3 %collective-permute-start.4 = (bf16[32,1024]{1,0:T(8,128)(2,1)S(1)}, bf16[32,1024]{1,0:T(8,128)(2,1)S(1)}, u32[]{:S(2)}, u32[]{:S(2)}) collective-permute-start(bf16[32,1024]{1,0:T(8,128)(2,1)S(1)} %collective-permute-done.2), channel_id=1, source_target_pairs={{0,14},{1,15},{2,0},{3,1},{4,2},{5,3},{6,4},{7,5},{8,6},{9,7},{10,... | collective-permute-start | bytes 196616 | tf_op jit(solution)/shard_map/ppermute | solution.py:38
  8.7 4.4 %collective-permute-start.5 = (bf16[32,1024]{1,0:T(8,128)(2,1)S(1)}, bf16[32,1024]{1,0:T(8,128)(2,1)S(1)}, u32[]{:S(2)}, u32[]{:S(2)}) collective-permute-start(bf16[32,1024]{1,0:T(8,128)(2,1)S(1)} %collective-permute-done.3), channel_id=1, source_target_pairs={{0,2},{1,3},{2,4},{3,5},{4,6},{5,7},{6,8},{7,9},{8,10},{9,11},{10,... | collective-permute-start | bytes 196616 | tf_op jit(solution)/shard_map/ppermute | solution.py:38
  9.9 4.7 %collective-permute-start.6 = (bf16[32,1024]{1,0:T(8,128)(2,1)S(1)}, bf16[32,1024]{1,0:T(8,128)(2,1)S(1)}, u32[]{:S(2)}, u32[]{:S(2)}) collective-permute-start(bf16[32,1024]{1,0:T(8,128)(2,1)S(1)} %collective-permute-done.4), channel_id=1, source_target_pairs={{0,14},{1,15},{2,0},{3,1},{4,2},{5,3},{6,4},{7,5},{8,6},{9,7},{10,... | collective-permute-start | bytes 196616 | tf_op jit(solution)/shard_map/ppermute | solution.py:38
  13.1 4.5 %collective-permute-start.7 = (bf16[32,1024]{1,0:T(8,128)(2,1)S(1)}, bf16[32,1024]{1,0:T(8,128)(2,1)S(1)}, u32[]{:S(2)}, u32[]{:S(2)}) collective-permute-start(bf16[32,1024]{1,0:T(8,128)(2,1)S(1)} %collective-permute-done.5), channel_id=1, source_target_pairs={{0,2},{1,3},{2,4},{3,5},{4,6},{5,7},{6,8},{7,9},{8,10},{9,11},{10,... | collective-permute-start | bytes 196616 | tf_op jit(solution)/shard_map/ppermute | solution.py:38
  17.7 9.6 %collective-permute-start.8 = (bf16[8,32,640]{2,1,0:T(8,128)(2,1)S(1)}, bf16[8,32,640]{2,1,0:T(8,128)(2,1)S(1)}, u32[]{:S(2)}, u32[]{:S(2)}) collective-permute-start(bf16[8,32,640]{2,1,0:T(8,128)(2,1)S(1)} %get-tuple-element.18), channel_id=1, source_target_pairs={{0,32},{1,33},{2,34},{3,35},{4,36},{5,37},{6,38},{7,39},{8,40},{9,... | collective-permute-start | bytes 983048 | tf_op jit(solution)/shard_map/ppermute | solution.py:38
  19.4 8.9 %collective-permute-start.9 = (bf16[8,32,640]{2,1,0:T(8,128)(2,1)S(1)}, bf16[8,32,640]{2,1,0:T(8,128)(2,1)S(1)}, u32[]{:S(2)}, u32[]{:S(2)}) collective-permute-start(bf16[8,32,640]{2,1,0:T(8,128)(2,1)S(1)} %get-tuple-element.18), channel_id=1, source_target_pairs={{0,33},{1,32},{2,35},{3,34},{4,37},{5,36},{6,39},{7,38},{8,41},{9,... | collective-permute-start | bytes 983048 | tf_op jit(solution)/shard_map/ppermute | solution.py:38
  27.4 9.1 %collective-permute-start.10 = (bf16[4,32,640]{2,1,0:T(8,128)(2,1)S(1)}, bf16[4,32,640]{2,1,0:T(8,128)(2,1)S(1)}, u32[]{:S(2)}, u32[]{:S(2)}) collective-permute-start(bf16[4,32,640]{2,1,0:T(8,128)(2,1)S(1)} %slice.57), channel_id=1, source_target_pairs={{0,32},{1,33},{2,34},{3,35},{4,36},{5,37},{6,38},{7,39},{8,40},{9,... | collective-permute-start | bytes 491528 | tf_op jit(solution)/shard_map/ppermute | solution.py:38
  28.3 8.2 %collective-permute-start.11 = (bf16[4,32,640]{2,1,0:T(8,128)(2,1)S(1)}, bf16[4,32,640]{2,1,0:T(8,128)(2,1)S(1)}, u32[]{:S(2)}, u32[]{:S(2)}) collective-permute-start(bf16[4,32,640]{2,1,0:T(8,128)(2,1)S(1)} %slice.58), channel_id=1, source_target_pairs={{0,33},{1,32},{2,35},{3,34},{4,37},{5,36},{6,39},{7,38},{8,41},{9,... | collective-permute-start | bytes 491528 | tf_op jit(solution)/shard_map/ppermute | solution.py:38
  36.5 80.7 %collective-permute-start = (bf16[256,4096]{1,0:T(8,128)(2,1)}, bf16[256,4096]{1,0:T(8,128)(2,1)}, u32[]{:S(2)}, u32[]{:S(2)}) collective-permute-start(bf16[256,4096]{1,0:T(8,128)(2,1)} %get-tuple-element.10), channel_id=1, source_target_pairs={{0,16},{1,17},{2,18},{3,19},{4,20},{5,21},{6,22},{7,23},{8,24},{9,... | collective-permute-start | bytes 6291464 | tf_op jit(solution)/shard_map/ppermute | solution.py:38
  36.8 47.1 %copy-start.1 = (bf16[4,8,32,640]{3,2,1,0:T(8,128)(2,1)}, bf16[4,8,32,640]{3,2,1,0:T(8,128)(2,1)S(1)}, u32[]{:S(2)}) copy-start(bf16[4,8,32,640]{3,2,1,0:T(8,128)(2,1)S(1)} %pad_maximum_fusion.refs_0_) | copy-start | bytes 3932164
  36.8 46.1 %collective-permute-start.12 = (bf16[4,8,32,640]{3,2,1,0:T(8,128)(2,1)S(1)}, bf16[4,8,32,640]{3,2,1,0:T(8,128)(2,1)S(1)}, u32[]{:S(2)}, u32[]{:S(2)}) collective-permute-start(bf16[4,8,32,640]{3,2,1,0:T(8,128)(2,1)S(1)} %pad_maximum_fusion.refs_0_), channel_id=1, source_target_pairs={{0,64},{1,65},{2,66},{3,67},{4,68},{5,69},{6,70},{7,71},{8,72},{9,... | collective-permute-start | bytes 3932168 | tf_op jit(solution)/shard_map/ppermute | solution.py:38
  38.4 46.2 %collective-permute-start.13 = (bf16[4,8,32,640]{3,2,1,0:T(8,128)(2,1)S(1)}, bf16[4,8,32,640]{3,2,1,0:T(8,128)(2,1)S(1)}, u32[]{:S(2)}, u32[]{:S(2)}) collective-permute-start(bf16[4,8,32,640]{3,2,1,0:T(8,128)(2,1)S(1)} %pad_maximum_fusion.refs_0_), channel_id=1, source_target_pairs={{0,192},{1,193},{2,194},{3,195},{4,196},{5,197},{6,198},{7,199},{8... | collective-permute-start | bytes 3932168 | tf_op jit(solution)/shard_map/ppermute | solution.py:38
  40.1 33.3 %collective-permute-start.16 = (bf16[8,32,384]{2,1,0:T(8,128)(2,1)S(1)}, bf16[8,32,384]{2,1,0:T(8,128)(2,1)S(1)}, u32[]{:S(2)}, u32[]{:S(2)}) collective-permute-start(bf16[8,32,384]{2,1,0:T(8,128)(2,1)S(1)} %get-tuple-element.16), channel_id=1, source_target_pairs={{0,64},{1,65},{2,66},{3,67},{4,68},{5,69},{6,70},{7,71},{8,72},{9,... | collective-permute-start | bytes 589832 | tf_op jit(solution)/shard_map/ppermute | solution.py:38
  40.7 33.2 %collective-permute-start.17 = (bf16[8,32,384]{2,1,0:T(8,128)(2,1)S(1)}, bf16[8,32,384]{2,1,0:T(8,128)(2,1)S(1)}, u32[]{:S(2)}, u32[]{:S(2)}) collective-permute-start(bf16[8,32,384]{2,1,0:T(8,128)(2,1)S(1)} %get-tuple-element.16), channel_id=1, source_target_pairs={{0,192},{1,193},{2,194},{3,195},{4,196},{5,197},{6,198},{7,199},{8... | collective-permute-start | bytes 589832 | tf_op jit(solution)/shard_map/ppermute | solution.py:38
  73.5 5.9 %collective-permute-start.18 = (bf16[4,32,384]{2,1,0:T(8,128)(2,1)S(1)}, bf16[4,32,384]{2,1,0:T(8,128)(2,1)S(1)}, u32[]{:S(2)}, u32[]{:S(2)}) collective-permute-start(bf16[4,32,384]{2,1,0:T(8,128)(2,1)S(1)} %slice.62), channel_id=1, source_target_pairs={{0,64},{1,65},{2,66},{3,67},{4,68},{5,69},{6,70},{7,71},{8,72},{9,... | collective-permute-start | bytes 294920 | tf_op jit(solution)/shard_map/ppermute | solution.py:38
  73.8 5.5 %collective-permute-start.19 = (bf16[4,32,384]{2,1,0:T(8,128)(2,1)S(1)}, bf16[4,32,384]{2,1,0:T(8,128)(2,1)S(1)}, u32[]{:S(2)}, u32[]{:S(2)}) collective-permute-start(bf16[4,32,384]{2,1,0:T(8,128)(2,1)S(1)} %slice.63), channel_id=1, source_target_pairs={{0,192},{1,193},{2,194},{3,195},{4,196},{5,197},{6,198},{7,199},{8... | collective-permute-start | bytes 294920 | tf_op jit(solution)/shard_map/ppermute | solution.py:38
  79.5 21.1 %copy-start.3 = (bf16[4,8,32,384]{3,2,1,0:T(8,128)(2,1)}, bf16[4,8,32,384]{3,2,1,0:T(8,128)(2,1)S(1)}, u32[]{:S(2)}) copy-start(bf16[4,8,32,384]{3,2,1,0:T(8,128)(2,1)S(1)} %pad_maximum_fusion.1.refs_5_) | copy-start | bytes 2359300
  79.6 24.3 %copy-start.9 = (bf16[2,2048,256]{2,1,0:T(8,128)(2,1)S(1)}, bf16[2,2048,256]{2,1,0:T(8,128)(2,1)}, u32[]{:S(2)}) copy-start(bf16[2,2048,256]{2,1,0:T(8,128)(2,1)} %param.8) | copy-start | bytes 6291460
  79.6 19.3 %collective-permute-start.20 = (bf16[4,8,32,384]{3,2,1,0:T(8,128)(2,1)S(1)}, bf16[4,8,32,384]{3,2,1,0:T(8,128)(2,1)S(1)}, u32[]{:S(2)}, u32[]{:S(2)}) collective-permute-start(bf16[4,8,32,384]{3,2,1,0:T(8,128)(2,1)S(1)} %pad_maximum_fusion.1.refs_5_), channel_id=1, source_target_pairs={{0,32},{1,33},{2,34},{3,35},{4,36},{5,37},{6,38},{7,39},{8,40},{9,... | collective-permute-start | bytes 2359304 | tf_op jit(solution)/shard_map/ppermute | solution.py:38
  79.7 20.1 %collective-permute-start.21 = (bf16[4,8,32,384]{3,2,1,0:T(8,128)(2,1)S(1)}, bf16[4,8,32,384]{3,2,1,0:T(8,128)(2,1)S(1)}, u32[]{:S(2)}, u32[]{:S(2)}) collective-permute-start(bf16[4,8,32,384]{3,2,1,0:T(8,128)(2,1)S(1)} %pad_maximum_fusion.1.refs_5_), channel_id=1, source_target_pairs={{0,33},{1,32},{2,35},{3,34},{4,37},{5,36},{6,39},{7,38},{8,41},{9,... | collective-permute-start | bytes 2359304 | tf_op jit(solution)/shard_map/ppermute | solution.py:38
  82.9 17.8 %copy-start.4 = (bf16[4,8,32,640]{3,2,1,0:T(8,128)(2,1)}, bf16[4,8,32,640]{3,2,1,0:T(8,128)(2,1)S(1)}, u32[]{:S(2)}) copy-start(bf16[4,8,32,640]{3,2,1,0:T(8,128)(2,1)S(1)} %collective-permute-done.12.refs_1_) | copy-start | bytes 3932164
  83.9 33.3 %collective-permute-start.14 = (bf16[2,8,32,640]{3,2,1,0:T(8,128)(2,1)}, bf16[2,8,32,640]{3,2,1,0:T(8,128)(2,1)}, u32[]{:S(2)}, u32[]{:S(2)}) collective-permute-start(bf16[2,8,32,640]{3,2,1,0:T(8,128)(2,1)} %slice.59), channel_id=1, source_target_pairs={{0,64},{1,65},{2,66},{3,67},{4,68},{5,69},{6,70},{7,71},{8,72},{9,... | collective-permute-start | bytes 1966088 | tf_op jit(solution)/shard_map/ppermute | solution.py:38
  84.5 19.4 %copy-start.5 = (bf16[4,8,32,640]{3,2,1,0:T(8,128)(2,1)}, bf16[4,8,32,640]{3,2,1,0:T(8,128)(2,1)S(1)}, u32[]{:S(2)}) copy-start(bf16[4,8,32,640]{3,2,1,0:T(8,128)(2,1)S(1)} %collective-permute-done.13.refs_2_) | copy-start | bytes 3932164
  84.6 32.6 %collective-permute-start.15 = (bf16[2,8,32,640]{3,2,1,0:T(8,128)(2,1)S(1)}, bf16[2,8,32,640]{3,2,1,0:T(8,128)(2,1)S(1)}, u32[]{:S(2)}, u32[]{:S(2)}) collective-permute-start(bf16[2,8,32,640]{3,2,1,0:T(8,128)(2,1)S(1)} %slice.60), channel_id=1, source_target_pairs={{0,192},{1,193},{2,194},{3,195},{4,196},{5,197},{6,198},{7,199},{8... | collective-permute-start | bytes 1966088 | tf_op jit(solution)/shard_map/ppermute | solution.py:38
  98.9 5.0 %copy-start.10 = (bf16[4,8,32,384]{3,2,1,0:T(8,128)(2,1)}, bf16[4,8,32,384]{3,2,1,0:T(8,128)(2,1)S(1)}, u32[]{:S(2)}) copy-start(bf16[4,8,32,384]{3,2,1,0:T(8,128)(2,1)S(1)} %collective-permute-done.20.refs_6_) | copy-start | bytes 2359300
  99.8 17.4 %collective-permute-start.22 = (bf16[2,8,32,384]{3,2,1,0:T(8,128)(2,1)}, bf16[2,8,32,384]{3,2,1,0:T(8,128)(2,1)}, u32[]{:S(2)}, u32[]{:S(2)}) collective-permute-start(bf16[2,8,32,384]{3,2,1,0:T(8,128)(2,1)} %slice.64), channel_id=1, source_target_pairs={{0,32},{1,33},{2,34},{3,35},{4,36},{5,37},{6,38},{7,39},{8,40},{9,... | collective-permute-start | bytes 1179656 | tf_op jit(solution)/shard_map/ppermute | solution.py:38
  99.8 4.1 %copy-start.11 = (bf16[4,8,32,384]{3,2,1,0:T(8,128)(2,1)}, bf16[4,8,32,384]{3,2,1,0:T(8,128)(2,1)S(1)}, u32[]{:S(2)}) copy-start(bf16[4,8,32,384]{3,2,1,0:T(8,128)(2,1)S(1)} %collective-permute-done.21.refs_7_) | copy-start | bytes 2359300
  100.7 16.5 %collective-permute-start.23 = (bf16[2,8,32,384]{3,2,1,0:T(8,128)(2,1)}, bf16[2,8,32,384]{3,2,1,0:T(8,128)(2,1)}, u32[]{:S(2)}, u32[]{:S(2)}) collective-permute-start(bf16[2,8,32,384]{3,2,1,0:T(8,128)(2,1)} %slice.65), channel_id=1, source_target_pairs={{0,33},{1,32},{2,35},{3,34},{4,37},{5,36},{6,39},{7,38},{8,41},{9,... | collective-permute-start | bytes 1179656 | tf_op jit(solution)/shard_map/ppermute | solution.py:38
  105.4 108.1 %all-to-all-start = ((bf16[16,2,128,256]{3,2,1,0:T(8,128)(2,1)}), bf16[16,2,128,256]{3,2,1,0:T(8,128)(2,1)S(1)}, u32[]{:S(2)}, u32[]{:S(2)}) async-start(bf16[16,2,128,256]{3,2,1,0:T(8,128)(2,1)} %bitcast.40), calls=%async_computation | async-start | bytes 4194304 | tf_op jit(solution)/shard_map/all_to_all | solution.py:306
  139.1 3.2 %copy-start.14 = (s32[128]{0:T(128)S(1)}, s32[128]{0:T(128)}, u32[]{:S(2)}) copy-start(s32[128]{0:T(128)} %param.9) | copy-start | bytes 1540
  142.3 2.9 collective-permute-start.24
  145.2 1.0 copy-start.12
  148.7 19.4 %collective-permute-start.25 = (bf16[128,1024]{1,0:T(8,128)(2,1)}, bf16[128,1024]{1,0:T(8,128)(2,1)S(1)}, u32[]{:S(2)}, u32[]{:S(2)}) collective-permute-start(bf16[128,1024]{1,0:T(8,128)(2,1)} %get-tuple-element.12), channel_id=1, source_target_pairs={{0,1},{1,0},{2,3},{3,2},{4,5},{5,4},{6,7},{7,6},{8,9},{9,8},{10,11... | collective-permute-start | bytes 786440 | tf_op jit(solution)/shard_map/ppermute | solution.py:38
  169.3 52.5 %copy-start.2 = (bf16[256,1024]{1,0:T(8,128)(2,1)}, bf16[256,1024]{1,0:T(8,128)(2,1)S(1)}, u32[]{:S(2)}) copy-start(bf16[256,1024]{1,0:T(8,128)(2,1)S(1)} %maximum_select_fusion.refs_0_.refs_8_) | copy-start | bytes 1572868
  169.3 13.7 %collective-permute-start.26 = (bf16[256,1024]{1,0:T(8,128)(2,1)S(1)}, bf16[256,1024]{1,0:T(8,128)(2,1)S(1)}, u32[]{:S(2)}, u32[]{:S(2)}) collective-permute-start(bf16[256,1024]{1,0:T(8,128)(2,1)S(1)} %maximum_select_fusion.refs_0_.refs_8_), channel_id=1, source_target_pairs={{0,2},{1,3},{2,4},{3,5},{4,6},{5,7},{6,8},{7,9},{8,10},{9,11},{10,... | collective-permute-start | bytes 1572872 | tf_op jit(solution)/shard_map/ppermute | solution.py:38
  169.4 14.0 %collective-permute-start.27 = (bf16[256,1024]{1,0:T(8,128)(2,1)S(1)}, bf16[256,1024]{1,0:T(8,128)(2,1)S(1)}, u32[]{:S(2)}, u32[]{:S(2)}) collective-permute-start(bf16[256,1024]{1,0:T(8,128)(2,1)S(1)} %maximum_select_fusion.refs_0_.refs_8_), channel_id=1, source_target_pairs={{0,14},{1,15},{2,0},{3,1},{4,2},{5,3},{6,4},{7,5},{8,6},{9,7},{10,... | collective-permute-start | bytes 1572872 | tf_op jit(solution)/shard_map/ppermute | solution.py:38
  183.0 38.8 %copy-start.6 = (bf16[256,1024]{1,0:T(8,128)(2,1)}, bf16[256,1024]{1,0:T(8,128)(2,1)S(1)}, u32[]{:S(2)}) copy-start(bf16[256,1024]{1,0:T(8,128)(2,1)S(1)} %collective-permute-done.26.refs_1_.refs_9_) | copy-start | bytes 1572868
  183.0 12.8 %collective-permute-start.28 = (bf16[256,1024]{1,0:T(8,128)(2,1)S(1)}, bf16[256,1024]{1,0:T(8,128)(2,1)S(1)}, u32[]{:S(2)}, u32[]{:S(2)}) collective-permute-start(bf16[256,1024]{1,0:T(8,128)(2,1)S(1)} %collective-permute-done.26.refs_1_.refs_9_), channel_id=1, source_target_pairs={{0,2},{1,3},{2,4},{3,5},{4,6},{5,7},{6,8},{7,9},{8,10},{9,11},{10,... | collective-permute-start | bytes 1572872 | tf_op jit(solution)/shard_map/ppermute | solution.py:38
  183.4 12.4 %copy-start.7 = (bf16[256,1024]{1,0:T(8,128)(2,1)}, bf16[256,1024]{1,0:T(8,128)(2,1)S(1)}, u32[]{:S(2)}) copy-start(bf16[256,1024]{1,0:T(8,128)(2,1)S(1)} %collective-permute-done.27.refs_2_.refs_10_) | copy-start | bytes 1572868
  183.4 14.2 %collective-permute-start.29 = (bf16[256,1024]{1,0:T(8,128)(2,1)S(1)}, bf16[256,1024]{1,0:T(8,128)(2,1)}, u32[]{:S(2)}, u32[]{:S(2)}) collective-permute-start(bf16[256,1024]{1,0:T(8,128)(2,1)S(1)} %collective-permute-done.27.refs_2_.refs_10_), channel_id=1, source_target_pairs={{0,14},{1,15},{2,0},{3,1},{4,2},{5,3},{6,4},{7,5},{8,6},{9,7},{10,... | collective-permute-start | bytes 1572872 | tf_op jit(solution)/shard_map/ppermute | solution.py:38
  195.8 1.8 copy-start.8
  195.8 13.4 %collective-permute-start.30 = (bf16[256,1024]{1,0:T(8,128)(2,1)S(1)}, bf16[256,1024]{1,0:T(8,128)(2,1)}, u32[]{:S(2)}, u32[]{:S(2)}) collective-permute-start(bf16[256,1024]{1,0:T(8,128)(2,1)S(1)} %collective-permute-done.28.refs_3_.refs_11_), channel_id=1, source_target_pairs={{0,2},{1,3},{2,4},{3,5},{4,6},{5,7},{6,8},{7,9},{8,10},{9,11},{10,... | collective-permute-start | bytes 1572872 | tf_op jit(solution)/shard_map/ppermute | solution.py:38
  197.6 15.9 %collective-permute-start.31 = (bf16[256,1024]{1,0:T(8,128)(2,1)}, bf16[256,1024]{1,0:T(8,128)(2,1)}, u32[]{:S(2)}, u32[]{:S(2)}) collective-permute-start(bf16[256,1024]{1,0:T(8,128)(2,1)} %collective-permute-done.29.refs_4_.refs_12_), channel_id=1, source_target_pairs={{0,14},{1,15},{2,0},{3,1},{4,2},{5,3},{6,4},{7,5},{8,6},{9,7},{10,... | collective-permute-start | bytes 1572872 | tf_op jit(solution)/shard_map/ppermute | solution.py:38
  209.2 12.6 %collective-permute-start.32 = (bf16[256,1024]{1,0:T(8,128)(2,1)}, bf16[256,1024]{1,0:T(8,128)(2,1)}, u32[]{:S(2)}, u32[]{:S(2)}) collective-permute-start(bf16[256,1024]{1,0:T(8,128)(2,1)} %collective-permute-done.30.refs_5_.refs_13_), channel_id=1, source_target_pairs={{0,2},{1,3},{2,4},{3,5},{4,6},{5,7},{6,8},{7,9},{8,10},{9,11},{10,... | collective-permute-start | bytes 1572872 | tf_op jit(solution)/shard_map/ppermute | solution.py:38
  213.5 8.3 %copy-start = (bf16[16,2,128,256]{3,2,1,0:T(8,128)(2,1)}, bf16[16,2,128,256]{3,2,1,0:T(8,128)(2,1)S(1)}, u32[]{:S(2)}) copy-start(bf16[16,2,128,256]{3,2,1,0:T(8,128)(2,1)S(1)} %all-to-all-done.q_ref) | copy-start | bytes 6291460
  (1 other events, 0.8 us)
